TPU v7x, 32 devices: a whole 2x2x4 slice. The times are simulated.
32 devices in a mesh: freq: 8 (over y, x, core), stn: 4 (over z).
Axes of the slice: x: 2, y: 2, z: 4, core: 2. Of those that a mesh axis runs over, the one named last changes fastest.
Arguments:
- voltages: bfloat16 [512, 16, 4096], P('stn', 'freq'), may hold values from -6 to 6
- filter_taps: float32 [16, 4096], replicated, may hold values from -1.5 to 1.5
- station_flags: int32 [256, 16], replicated, may hold values from 0 to 1, as said below
Outputs:
- visibilities: float32 [256, 512, 512], P('freq', 'stn')
Inputs may be any that keep to these rules, and one draw needn't show every extreme that they name: `station_flags`: 1 keeps a station's data in that spectrum, 0 flags it.
All inputs are finite; a program needn't handle non-finite values.
Results may differ from a plain program's by a relative error of at most 0.0039.
Values may be sent and summed in bfloat16 or wider, within the bound.
A program may use at most 192 MiB of HBM per device.

v0:
```python
import math

import jax
import jax.numpy as jnp
from jax import lax
from jax.sharding import PartitionSpec as P

AVG = 16


def from_behind(block, axis, distance):
    devices = range(lax.axis_size(axis))
    route = [(i - distance, i) for i in devices if i - distance in devices]
    return lax.ppermute(block, axis, route)


def dct_four(rows):
    highest = lax.Precision.HIGHEST
    count_rows, channels = rows.shape
    inner_len = 128
    outer_len = channels // inner_len
    positions = jnp.arange(channels).astype(jnp.float32)
    theta = math.pi * positions / (2 * channels)
    real_part = (rows * jnp.cos(theta)).reshape(count_rows, outer_len, inner_len)
    imag_part = (-rows * jnp.sin(theta)).reshape(count_rows, outer_len, inner_len)
    outer_idx = jnp.arange(outer_len, dtype=jnp.int32)
    outer_phase = (
        2
        * math.pi
        * (outer_idx[:, None] * outer_idx[None, :] % outer_len).astype(jnp.float32)
        / outer_len
    )
    outer_cos = jnp.cos(outer_phase)
    outer_sin = jnp.sin(outer_phase)
    section_real = jnp.einsum("pab,ak->pkb", real_part, outer_cos, precision=highest) + jnp.einsum(
        "pab,ak->pkb", imag_part, outer_sin, precision=highest
    )
    section_imag = jnp.einsum("pab,ak->pkb", imag_part, outer_cos, precision=highest) - jnp.einsum(
        "pab,ak->pkb", real_part, outer_sin, precision=highest
    )
    inner_idx = jnp.arange(inner_len, dtype=jnp.int32)
    twist_phase = (
        2 * math.pi * (outer_idx[:, None] * inner_idx[None, :]).astype(jnp.float32) / channels
    )
    twist_cos = jnp.cos(twist_phase)
    twist_sin = jnp.sin(twist_phase)
    twist_real = section_real * twist_cos + section_imag * twist_sin
    twist_imag = section_imag * twist_cos - section_real * twist_sin
    inner_phase = (
        2
        * math.pi
        * (inner_idx[:, None] * inner_idx[None, :] % inner_len).astype(jnp.float32)
        / inner_len
    )
    inner_cos = jnp.cos(inner_phase)
    inner_sin = jnp.sin(inner_phase)
    final_real = jnp.einsum("pkb,bq->pqk", twist_real, inner_cos, precision=highest) + jnp.einsum(
        "pkb,bq->pqk", twist_imag, inner_sin, precision=highest
    )
    final_imag = jnp.einsum("pkb,bq->pqk", twist_imag, inner_cos, precision=highest) - jnp.einsum(
        "pkb,bq->pqk", twist_real, inner_sin, precision=highest
    )
    final_real = final_real.reshape(count_rows, channels)
    final_imag = final_imag.reshape(count_rows, channels)
    post_angle = math.pi * (2 * positions + 1) / (4 * channels)
    return math.sqrt(2.0 / channels) * (
        final_real * jnp.cos(post_angle) + final_imag * jnp.sin(post_angle)
    )


def make_tile(mine, theirs):
    return jnp.einsum("gax,gbx->gab", mine, theirs, preferred_element_type=jnp.float32)


def body(voltages, filter_taps, station_flags):
    sig_dev, spec_dev, channels = voltages.shape
    tap_count = filter_taps.shape[0]
    history_len = tap_count - 1
    reach_count = -(-history_len // spec_dev)
    earlier = []
    for distance in range(1, reach_count + 1):
        needed = min(spec_dev, history_len - (distance - 1) * spec_dev)
        earlier.append(from_behind(voltages[:, spec_dev - needed :, :], "freq", distance))
    frames = jnp.concatenate(earlier[::-1] + [voltages], axis=1)
    window = jnp.zeros((sig_dev, spec_dev, channels), jnp.float32)
    for tap_index in range(tap_count):
        offset = history_len - tap_index
        window = window + filter_taps[tap_index][None, None, :] * frames[
            :, offset : offset + spec_dev, :
        ].astype(jnp.float32)
    channelized = dct_four(window.reshape(sig_dev * spec_dev, channels)).astype(jnp.bfloat16)
    groups_all = channels // AVG
    arranged = (
        channelized.reshape(sig_dev, spec_dev, groups_all, AVG)
        .transpose(2, 0, 1, 3)
        .reshape(groups_all, sig_dev, spec_dev * AVG)
    )
    turned = lax.all_to_all(arranged, "freq", split_axis=0, concat_axis=2, tiled=True)
    signal_flags = jnp.repeat(station_flags, 2, axis=0).astype(jnp.float32)
    position = lax.axis_index("stn")
    own_flags = lax.dynamic_slice_in_dim(signal_flags, position * sig_dev, sig_dev, 0)
    keep = jnp.repeat(own_flags, AVG, axis=1).astype(jnp.bfloat16)
    local = turned * keep[None]
    counts = jnp.dot(own_flags, signal_flags.T, precision=lax.Precision.HIGHEST)
    denominator = AVG * jnp.maximum(counts, 1.0)
    totals = make_tile(local, lax.all_gather(local, "stn", axis=1, tiled=True))
    return totals / denominator[None]


def solution(mesh):
    in_specs = (P("stn", "freq", None), P(), P())
    out_specs = P("freq", "stn", None)
    return jax.shard_map(body, mesh=mesh, in_specs=in_specs, out_specs=out_specs, check_vma=False)
```

profile of v0, /device:TPU:0, one launch (start us, length us, event | category | flops | bytes accessed | tf_op | source)
XLA Modules:
  0.0 650.6 jit_solution(14583448945114755904)
XLA Ops:
  6.5 2.6 collective-permute-start
  9.2 4.4 collective-permute-start.1
  13.6 4.1 slice.106
  17.7 1.1 copy.61
  18.8 0.7 collective-permute-start.7
  19.6 5.6 collective-permute-start.2
  25.2 2.6 collective-permute-start.3
  27.8 2.6 collective-permute-start.4
  30.4 30.8 %collective-permute-start.5 = (bf16[128,2,4096]{2,1,0:T(2,128)(2,1)S(1)}, bf16[128,2,4096]{2,1,0:T(2,128)(2,1)}, u32[]{:S(2)}, u32[]{:S(2)}) collective-permute-start(bf16[128,2,4096]{2,1,0:T(2,128)(2,1)S(1)} %copy-done.2), channel_id=1, source_target_pairs={{0,24},{4,28},{1,25},{5,29},{2,26},{6,30},{3,27},{7,31}} | collective-permute-start | bytes 6291464 | tf_op jit(solution)/shard_map/ppermute | solution.py:14
  61.2 1.3 copy-done.5
  62.6 45.0 %collective-permute-start.6 = (bf16[128,2,4096]{2,1,0:T(2,128)(2,1)S(1)}, bf16[128,2,4096]{2,1,0:T(2,128)(2,1)}, u32[]{:S(2)}, u32[]{:S(2)}) collective-permute-start(bf16[128,2,4096]{2,1,0:T(2,128)(2,1)S(1)} %copy-done.2), channel_id=1, source_target_pairs={{0,28},{1,29},{2,30},{3,31}} | collective-permute-start | bytes 6291464 | tf_op jit(solution)/shard_map/ppermute | solution.py:14
  107.5 0.1 fusion.52
  107.6 0.1 copy.50
  107.7 0.1 fusion.51
  107.8 0.1 copy.54
  107.9 0.1 fusion.55
  108.1 0.1 fusion.53
  108.2 2.6 fusion.98
  110.7 2.4 copy.46
  113.1 34.9 %collective-permute-done.3 = bf16[128,2,4096]{2,1,0:T(2,128)(2,1)} collective-permute-done((bf16[128,2,4096]{2,1,0:T(2,128)(2,1)S(1)}, bf16[128,2,4096]{2,1,0:T(2,128)(2,1)}, u32[]{:S(2)}, u32[]{:S(2)}) %collective-permute-start.3) | collective-permute-done | bytes 2097184 | tf_op jit(solution)/shard_map/ppermute | solution.py:14
  148.1 44.8 %collective-permute-done.4 = bf16[128,2,4096]{2,1,0:T(2,128)(2,1)} collective-permute-done((bf16[128,2,4096]{2,1,0:T(2,128)(2,1)S(1)}, bf16[128,2,4096]{2,1,0:T(2,128)(2,1)}, u32[]{:S(2)}, u32[]{:S(2)}) %collective-permute-start.4) | collective-permute-done | bytes 2097184 | tf_op jit(solution)/shard_map/ppermute | solution.py:14
  192.9 61.7 %multiply_add_fusion = f32[128,2,4096]{2,1,0:T(2,128)} fusion(bf16[128,2,4096]{2,1,0:T(2,128)(2,1)} %collective-permute-done.6, bf16[128,2,4096]{2,1,0:T(2,128)(2,1)} %collective-permute-done.5, bf16[128,2,4096]{2,1,0:T(2,128)(2,1)} %collective-permute-done.4, bf16[128,2,4096]{2,1,0:T(2,128)(2,1)} %collective-permute-done.3, ...), kind=kLoop, calls=%fused_computation.8 | loop fusion | flops 74448896 | bytes 22282240 | tf_op jit(solution)/shard_map/add | solution.py:88
  254.6 6.6 %reshape.108 = f32[256,32,128]{2,1,0:T(8,128)} reshape(f32[128,2,4096]{2,1,0:T(2,128)} %multiply_add_fusion) | data formatting | bytes 8388608 | tf_op jit(solution)/shard_map/reshape | solution.py:91
  261.2 6.0 fusion.14
  267.2 4.1 fusion.9
  271.3 4.4 fusion.20
  275.7 5.1 add_bitcast_fusion.1
  280.8 6.0 fusion.3
  286.8 8.3 %fusion.1 = f32[128,256,32]{1,0,2:T(8,128)} fusion(f32[256,32,128]{2,1,0:T(8,128)S(1)} %get-tuple-element.6), kind=kOutput, calls=%fused_computation.9 | convolution fusion | flops 1610842112 | bytes 8388608 | tf_op jit(solution)/shard_map/pkb,bq->pqk/dot_general | solution.py:60
  295.1 8.0 %add_bitcast_fusion = f32[256,128,32]{0,1,2:T(8,128)} fusion(f32[128,256,32]{1,0,2:T(8,128)S(1)} %fusion.3, f32[256,32,128]{2,1,0:T(8,128)S(1)} %get-tuple-element.5), kind=kOutput, calls=%fused_computation.4 | convolution fusion | flops 1611890688 | bytes 12582912 | tf_op jit(solution)/shard_map/pkb,bq->pqk/dot_general | solution.py:57
  303.1 14.5 %copy.49 = f32[256,128,32]{2,1,0:T(8,128)} copy(f32[256,128,32]{0,1,2:T(8,128)} %add_bitcast_fusion) | data formatting | bytes 8388608 | tf_op jit(solution)/shard_map/add | solution.py:57
  317.6 24.6 %reshape.109 = f32[128,2,256,16]{3,2,1,0:T(8,128)} reshape(f32[256,128,32]{2,1,0:T(8,128)} %copy.49) | data formatting | bytes 8388608 | tf_op jit(solution)/shard_map/reshape | solution.py:63
  342.3 11.4 %subtract_bitcast_fusion = f32[256,128,32]{0,1,2:T(8,128)} fusion(f32[128,256,32]{1,0,2:T(8,128)} %fusion.1, f32[256,32,128]{2,1,0:T(8,128)} %copy-done.1), kind=kOutput, calls=%fused_computation.3 | convolution fusion | flops 1611890688 | bytes 12582912 | tf_op jit(solution)/shard_map/pkb,bq->pqk/dot_general | solution.py:60
  353.7 14.5 %copy.53 = f32[256,128,32]{2,1,0:T(8,128)} copy(f32[256,128,32]{0,1,2:T(8,128)} %subtract_bitcast_fusion) | data formatting | bytes 8388608 | tf_op jit(solution)/shard_map/sub | solution.py:60
  368.2 24.4 %reshape.110 = f32[128,2,256,16]{3,2,1,0:T(8,128)} reshape(f32[256,128,32]{2,1,0:T(8,128)} %copy.53) | data formatting | bytes 8388608 | tf_op jit(solution)/shard_map/reshape | solution.py:64
  392.7 27.8 %fusion = bf16[256,128,2,16]{3,0,2,1:T(8,128)(2,1)} fusion(f32[128,2,256,16]{3,2,1,0:T(8,128)} %reshape.110, f32[128,2,256,16]{3,2,1,0:T(8,128)} %reshape.109, f32[256,16]{1,0:T(8,128)S(1)} %copy.54, f32[256,16]{1,0:T(8,128)S(1)} %copy.50), kind=kLoop, calls=%fused_computation.1 | loop fusion | flops 5242880 | bytes 10518528 | tf_op jit(solution)/shard_map/transpose | solution.py:95
  420.4 15.4 %copy.55 = bf16[256,128,2,16]{1,3,2,0:T(8,128)(2,1)} copy(bf16[256,128,2,16]{3,0,2,1:T(8,128)(2,1)} %fusion) | data formatting | bytes 4194304 | tf_op jit(solution)/shard_map/transpose | solution.py:95
  435.8 14.3 %all-to-all-start = ((bf16[256,128,32]{1,2,0:T(8,128)(2,1)}), bf16[256,128,32]{1,2,0:T(8,128)(2,1)S(1)}, u32[]{:S(2)}, u32[]{:S(2)}) async-start(bf16[256,128,32]{1,2,0:T(8,128)(2,1)} %bitcast.25), calls=%async_computation | async-start | bytes 4194304 | tf_op jit(solution)/shard_map/all_to_all | solution.py:98
  450.2 0.1 copy.57
  450.3 0.1 broadcast_in_dim.4
  450.5 0.1 copy.59
  450.6 26.1 %all-to-all-done = bf16[256,128,32]{1,2,0:T(8,128)(2,1)S(1)} async-done(((bf16[256,128,32]{1,2,0:T(8,128)(2,1)}), bf16[256,128,32]{1,2,0:T(8,128)(2,1)S(1)}, u32[]{:S(2)}, u32[]{:S(2)}) %all-to-all-start) | async-done | bytes 2097184 | tf_op jit(solution)/shard_map/all_to_all | solution.py:98
  476.7 1.9 copy.56
  478.7 3.5 copy.60
  482.2 1.5 broadcast_multiply_fusion
  483.8 0.4 fusion.27
  484.2 148.8 %all-gather.2.cloned.1.call-done = bf16[32,512,256]{2,1,0:T(8,128)(2,1)} async-done(((bf16[32,128,256]{2,1,0:T(8,128)(2,1)}), bf16[32,512,256]{2,1,0:T(8,128)(2,1)}) %all-gather.2.cloned.1.call-update) | async-done | bytes 8388624 | tf_op jit(solution)/shard_map/all_gather | solution.py:106
  633.0 10.3 %broadcast_divide_fusion = f32[32,128,512]{2,1,0:T(8,128)} fusion(f32[128,512]{1,0:T(8,128)S(1)} %fusion.27, bf16[32,128,256]{2,1,0:T(8,128)(2,1)} %broadcast_multiply_fusion, bf16[32,512,256]{2,1,0:T(8,128)(2,1)} %all-gather.2.cloned.1.call-done), kind=kOutput, calls=%fused_computation.2 | convolution fusion | flops 1075838976 | bytes 19136512 | tf_op jit(solution)/shard_map/gax,gbx->gab/dot_general | solution.py:72
  (26 shorter events, 0.3 us)
Async XLA Ops:
  6.5 13.0 %copy-start.2 = (bf16[128,2,4096]{2,1,0:T(2,128)(2,1)S(1)}, bf16[128,2,4096]{2,1,0:T(2,128)(2,1)}, u32[]{:S(2)}) copy-start(bf16[128,2,4096]{2,1,0:T(2,128)(2,1)} %param.3) | copy-start | bytes 6291460
  6.5 23.9 %collective-permute-start = (bf16[128,2,4096]{2,1,0:T(2,128)(2,1)}, bf16[128,2,4096]{2,1,0:T(2,128)(2,1)S(1)}, u32[]{:S(2)}, u32[]{:S(2)}) collective-permute-start(bf16[128,2,4096]{2,1,0:T(2,128)(2,1)} %param.3), channel_id=1, source_target_pairs={{0,4},{4,8},{8,12},{12,16},{16,20},{20,24},{24,28},{1,5},{5,9},{9,... | collective-permute-start | bytes 6291464 | tf_op jit(solution)/shard_map/ppermute | solution.py:14
  9.2 52.1 %collective-permute-start.1 = (bf16[128,2,4096]{2,1,0:T(2,128)(2,1)}, bf16[128,2,4096]{2,1,0:T(2,128)(2,1)S(1)}, u32[]{:S(2)}, u32[]{:S(2)}) collective-permute-start(bf16[128,2,4096]{2,1,0:T(2,128)(2,1)} %param.3), channel_id=1, source_target_pairs={{0,8},{4,12},{8,16},{12,20},{16,24},{20,28},{1,9},{5,13},{9,17},{1... | collective-permute-start | bytes 6291464 | tf_op jit(solution)/shard_map/ppermute | solution.py:14
  18.8 9.0 %collective-permute-start.7 = (bf16[128,1,4096]{2,0,1:T(8,128)(2,1)S(1)}, bf16[128,1,4096]{2,0,1:T(8,128)(2,1)S(1)}, u32[]{:S(2)}, u32[]{:S(2)}) collective-permute-start(bf16[128,1,4096]{2,0,1:T(8,128)(2,1)S(1)} %copy.61), channel_id=1, source_target_pairs={} | collective-permute-start | bytes 3145736 | tf_op jit(solution)/shard_map/ppermute | solution.py:14
  19.6 93.6 %collective-permute-start.2 = (bf16[128,2,4096]{2,1,0:T(2,128)(2,1)S(1)}, bf16[128,2,4096]{2,1,0:T(2,128)(2,1)}, u32[]{:S(2)}, u32[]{:S(2)}) collective-permute-start(bf16[128,2,4096]{2,1,0:T(2,128)(2,1)S(1)} %copy-done.2), channel_id=1, source_target_pairs={{0,12},{4,16},{8,20},{12,24},{16,28},{1,13},{5,17},{9,21},{13,25},... | collective-permute-start | bytes 6291464 | tf_op jit(solution)/shard_map/ppermute | solution.py:14
  25.2 122.9 %collective-permute-start.3 = (bf16[128,2,4096]{2,1,0:T(2,128)(2,1)S(1)}, bf16[128,2,4096]{2,1,0:T(2,128)(2,1)}, u32[]{:S(2)}, u32[]{:S(2)}) collective-permute-start(bf16[128,2,4096]{2,1,0:T(2,128)(2,1)S(1)} %copy-done.2), channel_id=1, source_target_pairs={{0,16},{4,20},{8,24},{12,28},{1,17},{5,21},{9,25},{13,29},{2,18},{... | collective-permute-start | bytes 6291464 | tf_op jit(solution)/shard_map/ppermute | solution.py:14
  27.8 165.1 %collective-permute-start.4 = (bf16[128,2,4096]{2,1,0:T(2,128)(2,1)S(1)}, bf16[128,2,4096]{2,1,0:T(2,128)(2,1)}, u32[]{:S(2)}, u32[]{:S(2)}) collective-permute-start(bf16[128,2,4096]{2,1,0:T(2,128)(2,1)S(1)} %copy-done.2), channel_id=1, source_target_pairs={{0,20},{4,24},{8,28},{1,21},{5,25},{9,29},{2,22},{6,26},{10,30},{3... | collective-permute-start | bytes 6291464 | tf_op jit(solution)/shard_map/ppermute | solution.py:14
  30.4 30.8 %copy-start.3 = (bf16[128,2,4096]{2,1,0:T(2,128)(2,1)}, bf16[128,2,4096]{2,1,0:T(2,128)(2,1)S(1)}, u32[]{:S(2)}) copy-start(bf16[128,2,4096]{2,1,0:T(2,128)(2,1)S(1)} %collective-permute-done) | copy-start | bytes 6291460
  30.4 162.5 %collective-permute-start.5 = (bf16[128,2,4096]{2,1,0:T(2,128)(2,1)S(1)}, bf16[128,2,4096]{2,1,0:T(2,128)(2,1)}, u32[]{:S(2)}, u32[]{:S(2)}) collective-permute-start(bf16[128,2,4096]{2,1,0:T(2,128)(2,1)S(1)} %copy-done.2), channel_id=1, source_target_pairs={{0,24},{4,28},{1,25},{5,29},{2,26},{6,30},{3,27},{7,31}} | collective-permute-start | bytes 6291464 | tf_op jit(solution)/shard_map/ppermute | solution.py:14
  61.2 1.3 copy-start.5
  62.6 130.4 %collective-permute-start.6 = (bf16[128,2,4096]{2,1,0:T(2,128)(2,1)S(1)}, bf16[128,2,4096]{2,1,0:T(2,128)(2,1)}, u32[]{:S(2)}, u32[]{:S(2)}) collective-permute-start(bf16[128,2,4096]{2,1,0:T(2,128)(2,1)S(1)} %copy-done.2), channel_id=1, source_target_pairs={{0,28},{1,29},{2,30},{3,31}} | collective-permute-start | bytes 6291464 | tf_op jit(solution)/shard_map/ppermute | solution.py:14
  107.9 85.0 %copy-start.4 = (bf16[128,2,4096]{2,1,0:T(2,128)(2,1)S(1)}, bf16[128,2,4096]{2,1,0:T(2,128)(2,1)}, u32[]{:S(2)}) copy-start(bf16[128,2,4096]{2,1,0:T(2,128)(2,1)} %copy-done.3) | copy-start | bytes 6291460
  261.2 6.0 copy-start
  280.8 14.3 %copy-start.1 = (f32[256,32,128]{2,1,0:T(8,128)}, f32[256,32,128]{2,1,0:T(8,128)S(1)}, u32[]{:S(2)}) copy-start(f32[256,32,128]{2,1,0:T(8,128)S(1)} %get-tuple-element.5) | copy-start | bytes 12582916
  435.8 14.3 %copy-start.6 = (s32[256,16]{0,1:T(8,128)S(1)}, s32[256,16]{0,1:T(8,128)}, u32[]{:S(2)}) copy-start(s32[256,16]{0,1:T(8,128)} %param.5) | copy-start | bytes 49156
  435.8 40.9 %all-to-all-start = ((bf16[256,128,32]{1,2,0:T(8,128)(2,1)}), bf16[256,128,32]{1,2,0:T(8,128)(2,1)S(1)}, u32[]{:S(2)}, u32[]{:S(2)}) async-start(bf16[256,128,32]{1,2,0:T(8,128)(2,1)} %bitcast.25), calls=%async_computation | async-start | bytes 4194304 | tf_op jit(solution)/shard_map/all_to_all | solution.py:98
  450.1 182.9 %all-gather.2.cloned.1.call-start = ((), (), s32[]{:S(2)}) async-start(), calls=%async_computation.1 | async-start | bytes 10485760 | tf_op jit(solution)/shard_map/all_gather | solution.py:106
Sparse Core Ops, SparseCore 0:
  483.9 149.0 all-gather.1
where the time goes:
time: 657 us; the launch traced here: 651 us
  waiting for transfers between devices  255 us (39%)
  local copies, waits for them, and re-layouts  118 us (18%)
  starting transfers between devices  109 us (17%)
  other arithmetic  91.4 us (14%)
  matrix products  63.9 us (10%)
  between operations  14.2 us (2%)
    all_gather x1, waiting for transfers between devices, body(): totals = make_tile(local, lax.all_gather(local, 'stn', axis=1, tiled=True))  149 us
    ppermute x8, starting transfers between devices, from_behind(): return lax.ppermute(block, axis, route)  94.4 us
    ppermute x8, waiting for transfers between devices, from_behind(): return lax.ppermute(block, axis, route)  79.8 us
    add x1, other arithmetic, body(): window + filter_taps[tap_index][None, None, :] * frames[:, offset:offset...  61.7 us
    transpose x1, other arithmetic, body(): arranged = channelized.reshape(sig_dev, spec_dev, groups_all, AVG).transp...  27.8 us
    all_to_all x1, waiting for transfers between devices, body(): lax.all_to_all(arranged, 'freq', split_axis=0, concat_axis=2, tiled=True)  26.1 us
    reshape x1, local copies, waits for them, and re-layouts, dct_four(): final_real = final_real.reshape(count_rows, channels)  24.6 us
    reshape x1, local copies, waits for them, and re-layouts, dct_four(): final_imag = final_imag.reshape(count_rows, channels)  24.4 us
  transfers between devices with their start and end apart: 10, of which 4 were waited for; matrix products, arithmetic and copies ran while one was open for 2% of the time, Pallas kernels for 0%

commit v1 on v0

--- a/solution.py
+++ b/solution.py
@@ -1,9 +1,18 @@
+import functools
 import math
 
 import jax
 import jax.numpy as jnp
+import ml_dtypes
+import numpy as np
 from jax import lax
+from jax.experimental import pallas as pl
+from jax.experimental.pallas import tpu as pltpu
 from jax.sharding import PartitionSpec as P
+
+MESH = pl.DeviceIdType.MESH
+LANES = 128
+ROWS = 16
 
 AVG = 16
 
@@ -72,7 +81,7 @@
     return jnp.einsum("gax,gbx->gab", mine, theirs, preferred_element_type=jnp.float32)
 
 
-def body(voltages, filter_taps, station_flags):
+def plain_body(voltages, filter_taps, station_flags):
     sig_dev, spec_dev, channels = voltages.shape
     tap_count = filter_taps.shape[0]
     history_len = tap_count - 1
@@ -107,7 +116,234 @@
     return totals / denominator[None]
 
 
+def dft_tables(channels):
+    sections = channels // AVG
+    k_low = np.arange(AVG)[:, None]
+    j_low = np.arange(sections)[None, :]
+    turn = 2 * np.pi / channels * (j_low * (k_low + 0.25) + k_low / 4 + 0.125)
+    scale = math.sqrt(2.0 / channels)
+    twist_cos = (scale * np.cos(turn)).astype(np.float32)
+    twist_sin = (scale * np.sin(turn)).astype(np.float32)
+    angle = 2 * np.pi / sections * (np.arange(sections)[:, None] * (j_low + 0.25))
+    full = np.concatenate([np.cos(angle), np.sin(angle)], axis=1)
+    high = full.astype(ml_dtypes.bfloat16)
+    low = (full - high.astype(np.float64)).astype(ml_dtypes.bfloat16)
+    return twist_cos, twist_sin, high, low
+
+
+def short_dft(pieces):
+    quarter = {}
+    for b in range(4):
+        for c in range(4):
+            real = pieces[b]
+            imag = None
+            for a in range(1, 4):
+                phase = 2 * math.pi * a * (c + 0.25) / 4
+                part = pieces[4 * a + b]
+                real = real + part * math.cos(phase)
+                term = part * -math.sin(phase)
+                imag = term if imag is None else imag + term
+            if b > 0:
+                phase = 2 * math.pi * b * (c + 0.25) / 16
+                co, si = math.cos(phase), math.sin(phase)
+                real, imag = real * co + imag * si, imag * co - real * si
+            quarter[b, c] = (real, imag)
+    out = [None] * 16
+    for c in range(4):
+        (r0, i0), (r1, i1), (r2, i2), (r3, i3) = (quarter[b, c] for b in range(4))
+        er, ei, fr, fi = r0 + r2, i0 + i2, r0 - r2, i0 - i2
+        gr, gi, hr, hi = r1 + r3, i1 + i3, r1 - r3, i1 - i3
+        out[c] = (er + gr, ei + gi)
+        out[c + 4] = (fr + hi, fi - hr)
+        out[c + 8] = (er - gr, ei - gi)
+        out[c + 12] = (fr - hi, fi + hr)
+    return out
+
+
+def channel_kernel(
+    n, volt_ref, taps_ref, keep_ref, tcos_ref, tsin_ref, high_ref, low_ref, out_ref,
+    frames, window, twist_high, twist_low, spectra, packed,
+    send_a, recv_a, send_b, recv_b, own_sem,
+):
+    me = lax.axis_index("freq")
+    spec_dev, _, channels = volt_ref.shape
+    tap_count = taps_ref.shape[0]
+    total = n * spec_dev
+    sections = channels // AVG
+    own_groups = sections // n
+    pitch = spectra.shape[1] // ROWS
+
+    barrier = pltpu.get_barrier_semaphore()
+    for step in range(1, n):
+        pl.semaphore_signal(
+            barrier, inc=1, device_id={"freq": lax.rem(me + step, n)}, device_id_type=MESH
+        )
+    pl.semaphore_wait(barrier, n - 1)
+
+    def signals_of(dev):
+        return pl.ds(pl.multiple_of(dev * ROWS, ROWS), ROWS)
+
+    copies = []
+    for step in range(1, n):
+        target = lax.rem(me + step, n)
+        copies.append(
+            pltpu.make_async_remote_copy(
+                src_ref=volt_ref.at[:, signals_of(target), :],
+                dst_ref=frames.at[me],
+                send_sem=send_a.at[step - 1],
+                recv_sem=recv_a.at[step - 1],
+                device_id={"freq": target},
+                device_id_type=MESH,
+            )
+        )
+    for copy in copies:
+        copy.start()
+    own = pltpu.make_async_copy(volt_ref.at[:, signals_of(me), :], frames.at[me], own_sem.at[0])
+    own.start()
+    own.wait()
+    for copy in copies:
+        copy.wait()
+
+    def filter_step(block, carry):
+        lanes = pl.ds(pl.multiple_of(block * LANES, LANES), LANES)
+        values = [
+            frames[m // spec_dev, m % spec_dev, :, lanes].astype(jnp.float32) for m in range(total)
+        ]
+        taps = taps_ref[:, lanes]
+        for m in range(total):
+            value = taps[0:1] * values[m]
+            for t in range(1, min(m + 1, tap_count)):
+                value = value + taps[t : t + 1] * values[m - t]
+            window[block, m * ROWS : (m + 1) * ROWS, :] = value
+        return carry
+
+    lax.fori_loop(0, channels // LANES, filter_step, 0)
+
+    contract = (((1,), (1,)), ((), ()))
+    halves = sections // LANES
+
+    def signal_step(s, carry):
+        for half in range(halves):
+            pieces = [
+                window[a * halves + half, pl.ds(s, total, stride=ROWS), :] for a in range(AVG)
+            ]
+            lanes = slice(half * LANES, (half + 1) * LANES)
+            for k, (real, imag) in enumerate(short_dft(pieces)):
+                co, si = tcos_ref[k : k + 1, lanes], tsin_ref[k : k + 1, lanes]
+                turned = (real * co + imag * si, imag * co - real * si)
+                rows = slice(k * total, (k + 1) * total)
+                for part, value in enumerate(turned):
+                    at = slice(part * sections + half * LANES, part * sections + (half + 1) * LANES)
+                    high = value.astype(jnp.bfloat16)
+                    twist_high[rows, at] = high
+                    twist_low[rows, at] = (value - high.astype(jnp.float32)).astype(jnp.bfloat16)
+        high = twist_high[...]
+        dot = functools.partial(
+            lax.dot_general, dimension_numbers=contract, preferred_element_type=jnp.float32
+        )
+        result = dot(high_ref[...], high) + (dot(low_ref[...], high) + dot(high_ref[...], twist_low[...]))
+        at = pl.ds(pl.multiple_of(s * pitch, 8), sections)
+        for part in range(AVG * total // LANES):
+            spectra[part, at, :] = result[:, part * LANES : (part + 1) * LANES]
+        return carry
+
+    lax.fori_loop(0, ROWS, signal_step, 0)
+
+    def pack_step(group, carry):
+        for part in range(AVG * total // LANES):
+            lanes = slice(part * LANES, (part + 1) * LANES)
+            value = spectra[part, pl.ds(group, ROWS, stride=pitch), :]
+            packed[group, :, lanes] = value.astype(jnp.bfloat16) * keep_ref[:, lanes]
+        return carry
+
+    lax.fori_loop(0, sections, pack_step, 0)
+
+    def groups_of(dev):
+        return pl.ds(dev * own_groups, own_groups)
+
+    copies = []
+    for step in range(1, n):
+        target = lax.rem(me + step, n)
+        copies.append(
+            pltpu.make_async_remote_copy(
+                src_ref=packed.at[groups_of(target)],
+                dst_ref=out_ref.at[:, signals_of(me), :],
+                send_sem=send_b.at[step - 1],
+                recv_sem=recv_b.at[step - 1],
+                device_id={"freq": target},
+                device_id_type=MESH,
+            )
+        )
+    for copy in copies:
+        copy.start()
+    own = pltpu.make_async_copy(
+        packed.at[groups_of(me)], out_ref.at[:, signals_of(me), :], own_sem.at[0]
+    )
+    own.start()
+    own.wait()
+    for copy in copies:
+        copy.wait()
+
+
+def channelize(n, turned, filter_taps, keep):
+    spec_dev, sig_dev, channels = turned.shape
+    sections = channels // AVG
+    total = n * spec_dev
+    width = AVG * total
+    pitch = sections + 8
+    vmem = pl.BlockSpec(memory_space=pltpu.VMEM)
+    any_space = pl.BlockSpec(memory_space=pl.ANY)
+    return pl.pallas_call(
+        functools.partial(channel_kernel, n),
+        out_shape=jax.ShapeDtypeStruct((sections // n, sig_dev, width), jnp.bfloat16),
+        in_specs=[any_space] + [vmem] * 6,
+        out_specs=any_space,
+        scratch_shapes=[
+            pltpu.VMEM((n, spec_dev, ROWS, channels), jnp.bfloat16),
+            pltpu.VMEM((channels // LANES, total * ROWS, LANES), jnp.float32),
+            pltpu.VMEM((width, 2 * sections), jnp.bfloat16),
+            pltpu.VMEM((width, 2 * sections), jnp.bfloat16),
+            pltpu.VMEM((width // LANES, ROWS * pitch, LANES), jnp.float32),
+            pltpu.VMEM((sections, ROWS, width), jnp.bfloat16),
+            pltpu.SemaphoreType.DMA((n - 1,)),
+            pltpu.SemaphoreType.DMA((n - 1,)),
+            pltpu.SemaphoreType.DMA((n - 1,)),
+            pltpu.SemaphoreType.DMA((n - 1,)),
+            pltpu.SemaphoreType.DMA((1,)),
+        ],
+        compiler_params=pltpu.CompilerParams(
+            collective_id=0, has_side_effects=True, vmem_limit_bytes=40 * 1024 * 1024
+        ),
+    )(turned, filter_taps, keep, *(jnp.asarray(table) for table in dft_tables(channels)))
+
+
+def body(n_freq, voltages, filter_taps, station_flags):
+    sig_dev, spec_dev, channels = voltages.shape
+    signal_flags = jnp.repeat(station_flags, 2, axis=0).astype(jnp.float32)
+    position = lax.axis_index("stn")
+    own_flags = lax.dynamic_slice_in_dim(signal_flags, position * sig_dev, sig_dev, 0)
+    mine = lax.dynamic_slice_in_dim(own_flags, lax.axis_index("freq") * ROWS, ROWS, 0)
+    keep = jnp.tile(mine, (1, AVG)).astype(jnp.bfloat16)
+    local = channelize(n_freq, voltages.transpose(1, 0, 2), filter_taps, keep)
+    counts = jnp.dot(own_flags, signal_flags.T, precision=lax.Precision.HIGHEST)
+    denominator = AVG * jnp.maximum(counts, 1.0)
+    totals = make_tile(local, lax.all_gather(local, "stn", axis=1, tiled=True))
+    return totals / denominator[None]
+
+
 def solution(mesh):
-    in_specs = (P("stn", "freq", None), P(), P())
-    out_specs = P("freq", "stn", None)
-    return jax.shard_map(body, mesh=mesh, in_specs=in_specs, out_specs=out_specs, check_vma=False)
+    n_freq = mesh.shape["freq"]
+
+    def whole(voltages, filter_taps, station_flags):
+        signals, spectra, channels = voltages.shape
+        even = signals == mesh.shape["stn"] * n_freq * ROWS
+        fits = even and spectra == ROWS and channels // AVG == 2 * LANES
+        inner = functools.partial(body, n_freq) if fits else plain_body
+        in_specs = (P("stn", "freq", None), P(), P())
+        out_specs = P("freq", "stn", None)
+        mapped = jax.shard_map(
+            inner, mesh=mesh, in_specs=in_specs, out_specs=out_specs, check_vma=False
+        )
+        return mapped(voltages, filter_taps, station_flags)
+
+    return whole

time: 657 us -> 253 us (0.39)
  local copies, waits for them, and re-layouts: 118 us -> 7.54 us
  starting transfers between devices: 109 us -> 0.01 us
  waiting for transfers between devices: 255 us -> 151 us
  other arithmetic: 91.4 us -> 0.72 us
  Pallas kernels: 0 us -> 69.3 us
  matrix products: 63.9 us -> 10.7 us
    ppermute x8 -> x0, starting transfers between devices: 94.4 us -> none  [from_behind(): return lax.ppermute(block, axis, route)]
    ppermute x8 -> x0, waiting for transfers between devices: 79.8 us -> none  [from_behind(): return lax.ppermute(block, axis, route)]
    pallas_call x0 -> x1, Pallas kernels: none -> 69.3 us  [channelize(): pl.pallas_call(functools.partial(channel_kernel, n), out_shape=jax.ShapeD...]
    add x1 -> x0, other arithmetic: 61.7 us -> none  [body(): window + filter_taps[tap_index][None, None, :] * frames[:, offset:offset...]
    reshape x3 -> x0, local copies, waits for them, and re-layouts: 55.7 us -> none  [the longest x1 24.6 us: dct_four(): final_real = final_real.reshape(count_rows, channels)]
    dot_general x8 -> x0, matrix products: 53.2 us -> none  [the longest x1 11.4 us: dct_four(): jnp.einsum('pkb,bq->pqk', twist_real, inner_sin, precision=highest)]
    transpose x1 -> x0, other arithmetic: 27.8 us -> none  [body(): arranged = channelized.reshape(sig_dev, spec_dev, groups_all, AVG).transp...]
    all_to_all x1 -> x0, waiting for transfers between devices: 26.1 us -> none  [body(): lax.all_to_all(arranged, 'freq', split_axis=0, concat_axis=2, tiled=True)]
  transfers between devices with their start and end apart: 10 -> 1, of which waited for: 4 -> 1; matrix products, arithmetic and copies ran while one was open for 2% -> 0% of each run, Pallas kernels for 0% -> 0%
where the time goes in v1:
time: 253 us
  waiting for transfers between devices  151 us (60%)
  Pallas kernels  69.3 us (27%)
  between operations  13.5 us (5%)
  matrix products  10.7 us (4%)
  local copies, waits for them, and re-layouts  7.54 us (3%)
    all_gather x1, waiting for transfers between devices, body(): totals = make_tile(local, lax.all_gather(local, 'stn', axis=1, tiled=True))  151 us
    pallas_call x1, Pallas kernels, channelize(): pl.pallas_call(functools.partial(channel_kernel, n), out_shape=jax.ShapeD...  69.3 us
    dot_general x1, matrix products, make_tile(): jnp.einsum('gax,gbx->gab', mine, theirs, preferred_element_type=jnp.float32)  10.3 us
    unnamed x11, local copies, waits for them, and re-layouts  7.2 us
  transfers between devices with their start and end apart: 1, of which 1 were waited for; matrix products, arithmetic and copies ran while one was open for 0% of the time, Pallas kernels for 0%

profile of v1, /device:TPU:0, one launch (start us, length us, event | category | flops | bytes accessed | tf_op | source)
XLA Modules:
  0.0 253.0 jit_solution(11340386672545289278)
XLA Ops:
  6.5 0.0 all-gather.2.cloned.1.call-start
  6.5 0.7 convert_element_type.12
  7.3 0.1 copy.9
  7.4 0.1 broadcast_in_dim.4
  7.5 0.1 convert_element_type.15.keep_ref
  7.6 2.9 %copy.11 = bf16[128,2,4096]{2,0,1:T(8,128)(2,1)S(1)} copy(bf16[128,2,4096]{2,1,0:T(2,128)(2,1)} %param.7) | data formatting | bytes 4194304 | tf_op args[0]
  10.6 0.0 copy-start
  10.6 0.9 copy-done
  11.5 0.0 copy-start.1
  11.5 0.9 copy-done.1
  12.5 0.0 copy-start.2
  12.5 0.9 copy-done.2
  13.4 0.0 copy-start.3
  13.4 0.7 copy-done.3
  14.1 0.0 copy-start.4
  14.1 0.7 copy-done.4
  14.8 69.3 %shard_map.73 = bf16[32,128,256]{2,1,0:T(8,128)(2,1)} custom-call(bf16[2,128,4096]{2,1,0:T(8,128)(2,1)S(1)} %bitcast.7, f32[16,4096]{1,0:T(8,128)S(1)} %copy-done, bf16[16,256]{1,0:T(8,128)(2,1)S(1)} %convert_element_type.15.keep_ref, f32[16,256]{1,0:T(8,128)S(1)} %copy-done.4, f32[16,256]{1,0:T(8,128)S(1)} %copy-done.3, bf16[256,512]{1,0:T(8,128)(2,1)S(1)} %copy-done.2, ...), custom_call_target="tpu_custom_call" | custom-call | tf_op jit(solution)/shard_map/pallas_call | solution.py:296
  84.2 0.0 all-gather.2.cloned.1.call-update
  84.2 0.4 fusion
  84.6 151.2 %all-gather.2.cloned.1.call-done = bf16[32,512,256]{2,1,0:T(8,128)(2,1)} async-done(((bf16[32,128,256]{2,1,0:T(8,128)(2,1)}), bf16[32,512,256]{2,1,0:T(8,128)(2,1)}) %all-gather.2.cloned.1.call-update) | async-done | bytes 8388624 | tf_op jit(solution)/shard_map/all_gather | solution.py:330
  235.8 10.3 %broadcast_divide_fusion = f32[32,128,512]{2,1,0:T(8,128)} fusion(f32[128,512]{1,0:T(8,128)S(1)} %fusion, bf16[32,128,256]{2,1,0:T(8,128)(2,1)} %shard_map.73, bf16[32,512,256]{2,1,0:T(8,128)(2,1)} %all-gather.2.cloned.1.call-done), kind=kOutput, calls=%fused_computation | convolution fusion | flops 1075838976 | bytes 19136512 | tf_op jit(solution)/shard_map/gax,gbx->gab/dot_general | solution.py:81
  (2 shorter events, 0.0 us)
Async XLA Ops:
  6.5 229.3 %all-gather.2.cloned.1.call-start = ((), (), s32[]{:S(2)}) async-start(), calls=%async_computation | async-start | bytes 10485760 | tf_op jit(solution)/shard_map/all_gather | solution.py:330
  10.6 1.0 copy-start
  11.5 0.9 copy-start.1
  12.5 0.9 copy-start.2
  13.4 0.7 copy-start.3
  14.1 0.7 copy-start.4
Sparse Core Ops, SparseCore 0:
  84.3 151.4 all-gather.1

commit v2 on v1

--- a/solution.py
+++ b/solution.py
@@ -13,6 +13,9 @@
 MESH = pl.DeviceIdType.MESH
 LANES = 128
 ROWS = 16
+N_STN = 4
+CHUNKS = 8
+LAG = 3
 
 AVG = 16
 
@@ -160,10 +163,10 @@
     return out
 
 
-def channel_kernel(
+def correlate_kernel(
     n, volt_ref, taps_ref, keep_ref, tcos_ref, tsin_ref, high_ref, low_ref, out_ref,
-    frames, window, twist_high, twist_low, spectra, packed,
-    send_a, recv_a, send_b, recv_b, own_sem,
+    frames, window, twist_high, twist_low, spectra, packed, blocks, tiles, sums,
+    send_a, recv_a, send_b, recv_b, own_b, send_x, recv_x, send_t, recv_t, out_sem, own_sem,
 ):
     me = lax.axis_index("freq")
     spec_dev, _, channels = volt_ref.shape
@@ -178,7 +181,14 @@
         pl.semaphore_signal(
             barrier, inc=1, device_id={"freq": lax.rem(me + step, n)}, device_id_type=MESH
         )
-    pl.semaphore_wait(barrier, n - 1)
+    for step in range(1, N_STN):
+        pl.semaphore_signal(
+            barrier,
+            inc=1,
+            device_id={"stn": lax.rem(lax.axis_index("stn") + step, N_STN)},
+            device_id_type=MESH,
+        )
+    pl.semaphore_wait(barrier, n - 1 + N_STN - 1)
 
     def signals_of(dev):
         return pl.ds(pl.multiple_of(dev * ROWS, ROWS), ROWS)
@@ -249,53 +259,191 @@
 
     lax.fori_loop(0, ROWS, signal_step, 0)
 
-    def pack_step(group, carry):
-        for part in range(AVG * total // LANES):
-            lanes = slice(part * LANES, (part + 1) * LANES)
-            value = spectra[part, pl.ds(group, ROWS, stride=pitch), :]
-            packed[group, :, lanes] = value.astype(jnp.bfloat16) * keep_ref[:, lanes]
+    chunk = own_groups // CHUNKS
+    stn = lax.axis_index("stn")
+
+    def part_of(index):
+        return pl.ds(pl.multiple_of(index * chunk, chunk), chunk)
+
+    def turn_copy(index, step):
+        target = lax.rem(me + step, n)
+        return pltpu.make_async_remote_copy(
+            src_ref=packed.at[pl.ds(target * own_groups + index * chunk, chunk)],
+            dst_ref=blocks.at[stn, part_of(index), signals_of(me), :],
+            send_sem=send_b.at[index, step - 1],
+            recv_sem=recv_b.at[index, step - 1],
+            device_id={"freq": target},
+            device_id_type=MESH,
+        )
+
+    def own_copy(index):
+        return pltpu.make_async_copy(
+            packed.at[pl.ds(me * own_groups + index * chunk, chunk)],
+            blocks.at[stn, part_of(index), signals_of(me), :],
+            own_b.at[index],
+        )
+
+    def pack_chunk(index, carry):
+        def pack_step(at, inner):
+            group = (at // chunk) * own_groups + index * chunk + at % chunk
+            for part in range(AVG * total // LANES):
+                lanes = slice(part * LANES, (part + 1) * LANES)
+                value = spectra[part, pl.ds(group, ROWS, stride=pitch), :]
+                packed[group, :, lanes] = value.astype(jnp.bfloat16) * keep_ref[:, lanes]
+            return inner
+
+        lax.fori_loop(0, n * chunk, pack_step, 0)
+        for step in range(1, n):
+            turn_copy(index, step).start()
+        own_copy(index).start()
         return carry
 
-    lax.fori_loop(0, sections, pack_step, 0)
-
-    def groups_of(dev):
-        return pl.ds(dev * own_groups, own_groups)
-
-    copies = []
-    for step in range(1, n):
-        target = lax.rem(me + step, n)
-        copies.append(
-            pltpu.make_async_remote_copy(
-                src_ref=packed.at[groups_of(target)],
-                dst_ref=out_ref.at[:, signals_of(me), :],
-                send_sem=send_b.at[step - 1],
-                recv_sem=recv_b.at[step - 1],
-                device_id={"freq": target},
-                device_id_type=MESH,
-            )
-        )
-    for copy in copies:
-        copy.start()
-    own = pltpu.make_async_copy(
-        packed.at[groups_of(me)], out_ref.at[:, signals_of(me), :], own_sem.at[0]
-    )
-    own.start()
-    own.wait()
-    for copy in copies:
-        copy.wait()
-
-
-def channelize(n, turned, filter_taps, keep):
+    lax.fori_loop(0, CHUNKS, pack_chunk, 0)
+
+    def own_ready(index):
+        for step in range(1, n):
+            turn_copy(index, step).wait_recv()
+        own_copy(index).wait()
+
+    def block_copy(owner, index, send, recv, target):
+        return pltpu.make_async_remote_copy(
+            src_ref=blocks.at[owner, part_of(index)],
+            dst_ref=blocks.at[owner, part_of(index)],
+            send_sem=send_x.at[send, index],
+            recv_sem=recv_x.at[recv, index],
+            device_id={"stn": target},
+            device_id_type=MESH,
+        )
+
+    def tile_copy(place, index, target):
+        return pltpu.make_async_remote_copy(
+            src_ref=tiles.at[place, part_of(index)],
+            dst_ref=tiles.at[place, part_of(index)],
+            send_sem=send_t.at[place, index],
+            recv_sem=recv_t.at[place, index],
+            device_id={"stn": target},
+            device_id_type=MESH,
+        )
+
+    def out_copy(index):
+        return pltpu.make_async_copy(
+            sums.at[part_of(index)], out_ref.at[part_of(index)], out_sem.at[index]
+        )
+
+    def columns_of(owner):
+        return pl.ds(pl.multiple_of(owner * LANES, LANES), LANES)
+
+    def product(left, right, group):
+        return lax.dot_general(
+            blocks[left, group], blocks[right, group], contract, preferred_element_type=jnp.float32
+        )
+
+    def own_tile(owner, index):
+        for i in range(chunk):
+            group = index * chunk + i
+            sums[group, :, columns_of(owner)] = product(stn, owner, group)
+
+    def end_tile(end, owner, place, index):
+        for i in range(chunk):
+            group = index * chunk + i
+            tiles[place, group] = product(end, owner, group).astype(jnp.bfloat16)
+        tile_copy(place, index, end).start()
+
+    last = N_STN - 1
+
+    @pl.when((stn == 0) | (stn == last))
+    def _():
+        near = 1 + stn // last
+
+        def send_step(index, carry):
+            own_ready(index)
+            block_copy(stn, index, 0, 0, near).start()
+            own_tile(stn, index)
+            return carry
+
+        def take_step(index, carry):
+            for place, owner in enumerate((near, last - near, last - stn)):
+                tile_copy(place, index, near).wait_recv()
+                for i in range(chunk):
+                    group = index * chunk + i
+                    sums[group, :, columns_of(owner)] = tiles[place, group].astype(jnp.float32)
+            out_copy(index).start()
+            return carry
+
+        def drain_step(index, carry):
+            block_copy(stn, index, 0, 0, near).wait_send()
+            out_copy(index).wait()
+            return carry
+
+        lax.fori_loop(0, CHUNKS, send_step, 0)
+        lax.fori_loop(0, CHUNKS, take_step, 0)
+        lax.fori_loop(0, CHUNKS, drain_step, 0)
+
+    @pl.when((stn > 0) & (stn < last))
+    def _():
+        end = (stn - 1) * last
+        across = last - stn
+        far = last - end
+
+        def step_all(step, carry):
+            @pl.when(step < CHUNKS)
+            def _():
+                own_ready(step)
+                block_copy(stn, step, 0, 1, across).start()
+
+            @pl.when((step >= 1) & (step < CHUNKS + 1))
+            def _():
+                index = step - 1
+                block_copy(end, index, 1, 0, across).wait_recv()
+                block_copy(end, index, 1, 2, across).start()
+                end_tile(end, stn, 0, index)
+                own_tile(stn, index)
+                own_tile(end, index)
+
+            @pl.when(step >= LAG)
+            def _():
+                index = step - LAG
+                block_copy(across, index, 0, 1, across).wait_recv()
+                end_tile(end, across, 1, index)
+                own_tile(across, index)
+                block_copy(far, index, 1, 2, across).wait_recv()
+                end_tile(end, far, 2, index)
+                own_tile(far, index)
+                out_copy(index).start()
+
+            return carry
+
+        def drain_step(index, carry):
+            block_copy(stn, index, 0, 1, across).wait_send()
+            block_copy(end, index, 1, 2, across).wait_send()
+            for place in range(3):
+                tile_copy(place, index, end).wait_send()
+            out_copy(index).wait()
+            return carry
+
+        lax.fori_loop(0, CHUNKS + LAG, step_all, 0)
+        lax.fori_loop(0, CHUNKS, drain_step, 0)
+
+    def finish_step(index, carry):
+        for step in range(1, n):
+            turn_copy(index, step).wait_send()
+        return carry
+
+    lax.fori_loop(0, CHUNKS, finish_step, 0)
+
+
+def correlate(n, turned, filter_taps, keep):
     spec_dev, sig_dev, channels = turned.shape
     sections = channels // AVG
     total = n * spec_dev
     width = AVG * total
+    groups = sections // n
     pitch = sections + 8
     vmem = pl.BlockSpec(memory_space=pltpu.VMEM)
     any_space = pl.BlockSpec(memory_space=pl.ANY)
     return pl.pallas_call(
-        functools.partial(channel_kernel, n),
-        out_shape=jax.ShapeDtypeStruct((sections // n, sig_dev, width), jnp.bfloat16),
+        functools.partial(correlate_kernel, n),
+        out_shape=jax.ShapeDtypeStruct((groups, sig_dev, N_STN * sig_dev), jnp.float32),
         in_specs=[any_space] + [vmem] * 6,
         out_specs=any_space,
         scratch_shapes=[
@@ -305,14 +453,23 @@
             pltpu.VMEM((width, 2 * sections), jnp.bfloat16),
             pltpu.VMEM((width // LANES, ROWS * pitch, LANES), jnp.float32),
             pltpu.VMEM((sections, ROWS, width), jnp.bfloat16),
+            pltpu.VMEM((N_STN, groups, sig_dev, width), jnp.bfloat16),
+            pltpu.VMEM((N_STN - 1, groups, sig_dev, sig_dev), jnp.bfloat16),
+            pltpu.VMEM((groups, sig_dev, N_STN * sig_dev), jnp.float32),
             pltpu.SemaphoreType.DMA((n - 1,)),
             pltpu.SemaphoreType.DMA((n - 1,)),
-            pltpu.SemaphoreType.DMA((n - 1,)),
-            pltpu.SemaphoreType.DMA((n - 1,)),
+            pltpu.SemaphoreType.DMA((CHUNKS, n - 1)),
+            pltpu.SemaphoreType.DMA((CHUNKS, n - 1)),
+            pltpu.SemaphoreType.DMA((CHUNKS,)),
+            pltpu.SemaphoreType.DMA((2, CHUNKS)),
+            pltpu.SemaphoreType.DMA((3, CHUNKS)),
+            pltpu.SemaphoreType.DMA((3, CHUNKS)),
+            pltpu.SemaphoreType.DMA((3, CHUNKS)),
+            pltpu.SemaphoreType.DMA((CHUNKS,)),
             pltpu.SemaphoreType.DMA((1,)),
         ],
         compiler_params=pltpu.CompilerParams(
-            collective_id=0, has_side_effects=True, vmem_limit_bytes=40 * 1024 * 1024
+            collective_id=0, has_side_effects=True, vmem_limit_bytes=52 * 1024 * 1024
         ),
     )(turned, filter_taps, keep, *(jnp.asarray(table) for table in dft_tables(channels)))
 
@@ -324,10 +481,9 @@
     own_flags = lax.dynamic_slice_in_dim(signal_flags, position * sig_dev, sig_dev, 0)
     mine = lax.dynamic_slice_in_dim(own_flags, lax.axis_index("freq") * ROWS, ROWS, 0)
     keep = jnp.tile(mine, (1, AVG)).astype(jnp.bfloat16)
-    local = channelize(n_freq, voltages.transpose(1, 0, 2), filter_taps, keep)
+    totals = correlate(n_freq, voltages.transpose(1, 0, 2), filter_taps, keep)
     counts = jnp.dot(own_flags, signal_flags.T, precision=lax.Precision.HIGHEST)
     denominator = AVG * jnp.maximum(counts, 1.0)
-    totals = make_tile(local, lax.all_gather(local, "stn", axis=1, tiled=True))
     return totals / denominator[None]
 
 
@@ -337,6 +493,7 @@
     def whole(voltages, filter_taps, station_flags):
         signals, spectra, channels = voltages.shape
         even = signals == mesh.shape["stn"] * n_freq * ROWS
+        even = even and mesh.shape["stn"] == N_STN and n_freq * ROWS == LANES
         fits = even and spectra == ROWS and channels // AVG == 2 * LANES
         inner = functools.partial(body, n_freq) if fits else plain_body
         in_specs = (P("stn", "freq", None), P(), P())

time: 253 us -> 169 us (0.67)
  waiting for transfers between devices: 151 us -> 0 us
  Pallas kernels: 69.3 us -> 150 us
  between operations: 13.5 us -> 0.04 us
  matrix products: 10.7 us -> 0.39 us
  other arithmetic: 0.72 us -> 9.19 us
    all_gather x1 -> x0, waiting for transfers between devices: 151 us -> none  [body(): totals = make_tile(local, lax.all_gather(local, 'stn', axis=1, tiled=True))]
    pallas_call x1, Pallas kernels: 69.3 us -> 150 us  [correlate(): pl.pallas_call(functools.partial(correlate_kernel, n), out_shape=jax.Shap...]
    dot_general x1 -> x0, matrix products: 10.3 us -> none  [make_tile(): jnp.einsum('gax,gbx->gab', mine, theirs, preferred_element_type=jnp.float32)]
    div x0 -> x1, other arithmetic: none -> 8.47 us  [body(): return totals / denominator[None]]
  transfers between devices with their start and end apart: 1 -> 0, of which waited for: 1 -> 0; matrix products, arithmetic and copies ran while one was open for 0% -> 0% of each run, Pallas kernels for 0% -> 0%
where the time goes in v2:
time: 169 us
  Pallas kernels  150 us (89%)
  other arithmetic  9.19 us (5%)
  local copies, waits for them, and re-layouts  8.86 us (5%)
    pallas_call x1, Pallas kernels, correlate(): pl.pallas_call(functools.partial(correlate_kernel, n), out_shape=jax.Shap...  150 us
    unnamed x11, local copies, waits for them, and re-layouts  8.52 us
    div x1, other arithmetic, body(): return totals / denominator[None]  8.47 us

profile of v2, /device:TPU:0, one launch (start us, length us, event | category | flops | bytes accessed | tf_op | source)
XLA Modules:
  0.0 168.7 jit_solution(11229733526897318247)
XLA Ops:
  0.0 0.7 convert_element_type.12
  0.7 0.1 copy.9
  0.8 0.1 broadcast_in_dim.4
  0.9 0.4 fusion
  1.4 0.1 convert_element_type.15.keep_ref
  1.5 4.2 %copy.11 = bf16[128,2,4096]{2,0,1:T(8,128)(2,1)} copy(bf16[128,2,4096]{2,1,0:T(2,128)(2,1)} %param.7) | data formatting | bytes 4194304 | tf_op args[0]
  5.7 0.0 copy-start
  5.7 0.9 copy-done
  6.7 0.0 copy-start.1
  6.7 0.9 copy-done.1
  7.6 0.0 copy-start.2
  7.6 0.9 copy-done.2
  8.6 0.0 copy-start.3
  8.6 0.7 copy-done.3
  9.3 0.0 copy-start.4
  9.3 0.7 copy-done.4
  10.0 150.2 %shard_map.73 = f32[32,128,512]{2,1,0:T(8,128)} custom-call(bf16[2,128,4096]{2,1,0:T(8,128)(2,1)} %bitcast.5, f32[16,4096]{1,0:T(8,128)S(1)} %copy-done, bf16[16,256]{1,0:T(8,128)(2,1)S(1)} %convert_element_type.15.keep_ref, f32[16,256]{1,0:T(8,128)S(1)} %copy-done.4, f32[16,256]{1,0:T(8,128)S(1)} %copy-done.3, bf16[256,512]{1,0:T(8,128)(2,1)S(1)} %copy-done.2, ...), custom_call_target="tpu_custom_call" | custom-call | tf_op jit(solution)/shard_map/pallas_call | solution.py:444
  160.2 8.5 %broadcast_divide_fusion = f32[32,128,512]{2,1,0:T(8,128)} fusion(f32[32,128,512]{2,1,0:T(8,128)} %shard_map.73, f32[128,512]{1,0:T(8,128)S(1)} %fusion), kind=kLoop, calls=%fused_computation | loop fusion | flops 2097152 | bytes 17039360 | tf_op jit(solution)/shard_map/div | solution.py:487
  (2 shorter events, 0.0 us)
Async XLA Ops:
  5.7 0.9 copy-start
  6.7 0.9 copy-start.1
  7.6 0.9 copy-start.2
  8.6 0.7 copy-start.3
  9.3 0.7 copy-start.4

commit v3 on v2

--- a/solution.py
+++ b/solution.py
@@ -16,6 +16,7 @@
 N_STN = 4
 CHUNKS = 8
 LAG = 3
+PIECES = 4
 
 AVG = 16
 
@@ -163,11 +164,18 @@
     return out
 
 
-def correlate_kernel(
-    n, volt_ref, taps_ref, keep_ref, tcos_ref, tsin_ref, high_ref, low_ref, out_ref,
-    frames, window, twist_high, twist_low, spectra, packed, blocks, tiles, sums,
-    send_a, recv_a, send_b, recv_b, own_b, send_x, recv_x, send_t, recv_t, out_sem, own_sem,
-):
+def correlate_kernel(n, volt_ref, *refs):
+    given, (out_ref, *held), rest = refs[:6], refs[6:13], refs[13:]
+    (frames, window, twist_high, twist_low, spectra, packed, blocks, tiles, sums) = rest[:9]
+    (send_a, recv_a, send_b, recv_b, own_b, send_x, recv_x, send_t, recv_t) = rest[9:18]
+    out_sem, own_sem, given_sem = rest[18:]
+    taps_ref, keep_ref, tcos_ref, tsin_ref, high_ref, low_ref = held
+    loads = [
+        pltpu.make_async_copy(src, dst, given_sem.at[at])
+        for at, (src, dst) in enumerate(zip(given, held, strict=True))
+    ]
+    for load in loads:
+        load.start()
     me = lax.axis_index("freq")
     spec_dev, _, channels = volt_ref.shape
     tap_count = taps_ref.shape[0]
@@ -193,26 +201,28 @@
     def signals_of(dev):
         return pl.ds(pl.multiple_of(dev * ROWS, ROWS), ROWS)
 
-    copies = []
-    for step in range(1, n):
+    piece = channels // PIECES
+
+    def volt_copy(index, step):
         target = lax.rem(me + step, n)
-        copies.append(
-            pltpu.make_async_remote_copy(
-                src_ref=volt_ref.at[:, signals_of(target), :],
-                dst_ref=frames.at[me],
-                send_sem=send_a.at[step - 1],
-                recv_sem=recv_a.at[step - 1],
-                device_id={"freq": target},
-                device_id_type=MESH,
-            )
-        )
-    for copy in copies:
-        copy.start()
+        lanes = pl.ds(pl.multiple_of(index * piece, piece), piece)
+        return pltpu.make_async_remote_copy(
+            src_ref=volt_ref.at[:, signals_of(target), lanes],
+            dst_ref=frames.at[me, :, :, lanes],
+            send_sem=send_a.at[index, step - 1],
+            recv_sem=recv_a.at[index, step - 1],
+            device_id={"freq": target},
+            device_id_type=MESH,
+        )
+
+    for index in range(PIECES):
+        for step in range(1, n):
+            volt_copy(index, step).start()
     own = pltpu.make_async_copy(volt_ref.at[:, signals_of(me), :], frames.at[me], own_sem.at[0])
     own.start()
+    for load in loads:
+        load.wait()
     own.wait()
-    for copy in copies:
-        copy.wait()
 
     def filter_step(block, carry):
         lanes = pl.ds(pl.multiple_of(block * LANES, LANES), LANES)
@@ -227,7 +237,13 @@
             window[block, m * ROWS : (m + 1) * ROWS, :] = value
         return carry
 
-    lax.fori_loop(0, channels // LANES, filter_step, 0)
+    def filter_piece(index, carry):
+        for step in range(1, n):
+            volt_copy(index, step).wait_recv()
+        blocks_in = piece // LANES
+        return lax.fori_loop(index * blocks_in, (index + 1) * blocks_in, filter_step, carry)
+
+    lax.fori_loop(0, PIECES, filter_piece, 0)
 
     contract = (((1,), (1,)), ((), ()))
     halves = sections // LANES
@@ -341,7 +357,7 @@
     def own_tile(owner, index):
         for i in range(chunk):
             group = index * chunk + i
-            sums[group, :, columns_of(owner)] = product(stn, owner, group)
+            sums[group, :, columns_of(owner)] = product(stn, owner, group).astype(jnp.bfloat16)
 
     def end_tile(end, owner, place, index):
         for i in range(chunk):
@@ -366,7 +382,7 @@
                 tile_copy(place, index, near).wait_recv()
                 for i in range(chunk):
                     group = index * chunk + i
-                    sums[group, :, columns_of(owner)] = tiles[place, group].astype(jnp.float32)
+                    sums[group, :, columns_of(owner)] = tiles[place, group]
             out_copy(index).start()
             return carry
 
@@ -424,6 +440,10 @@
         lax.fori_loop(0, CHUNKS + LAG, step_all, 0)
         lax.fori_loop(0, CHUNKS, drain_step, 0)
 
+    for index in range(PIECES):
+        for step in range(1, n):
+            volt_copy(index, step).wait_send()
+
     def finish_step(index, carry):
         for step in range(1, n):
             turn_copy(index, step).wait_send()
@@ -439,14 +459,15 @@
     width = AVG * total
     groups = sections // n
     pitch = sections + 8
-    vmem = pl.BlockSpec(memory_space=pltpu.VMEM)
     any_space = pl.BlockSpec(memory_space=pl.ANY)
+    tables = (filter_taps, keep, *(jnp.asarray(table) for table in dft_tables(channels)))
     return pl.pallas_call(
         functools.partial(correlate_kernel, n),
-        out_shape=jax.ShapeDtypeStruct((groups, sig_dev, N_STN * sig_dev), jnp.float32),
-        in_specs=[any_space] + [vmem] * 6,
+        out_shape=jax.ShapeDtypeStruct((groups, sig_dev, N_STN * sig_dev), jnp.bfloat16),
+        in_specs=[any_space] * 7,
         out_specs=any_space,
-        scratch_shapes=[
+        scratch_shapes=[pltpu.VMEM(table.shape, table.dtype) for table in tables]
+        + [
             pltpu.VMEM((n, spec_dev, ROWS, channels), jnp.bfloat16),
             pltpu.VMEM((channels // LANES, total * ROWS, LANES), jnp.float32),
             pltpu.VMEM((width, 2 * sections), jnp.bfloat16),
@@ -455,9 +476,9 @@
             pltpu.VMEM((sections, ROWS, width), jnp.bfloat16),
             pltpu.VMEM((N_STN, groups, sig_dev, width), jnp.bfloat16),
             pltpu.VMEM((N_STN - 1, groups, sig_dev, sig_dev), jnp.bfloat16),
-            pltpu.VMEM((groups, sig_dev, N_STN * sig_dev), jnp.float32),
-            pltpu.SemaphoreType.DMA((n - 1,)),
-            pltpu.SemaphoreType.DMA((n - 1,)),
+            pltpu.VMEM((groups, sig_dev, N_STN * sig_dev), jnp.bfloat16),
+            pltpu.SemaphoreType.DMA((PIECES, n - 1)),
+            pltpu.SemaphoreType.DMA((PIECES, n - 1)),
             pltpu.SemaphoreType.DMA((CHUNKS, n - 1)),
             pltpu.SemaphoreType.DMA((CHUNKS, n - 1)),
             pltpu.SemaphoreType.DMA((CHUNKS,)),
@@ -467,11 +488,12 @@
             pltpu.SemaphoreType.DMA((3, CHUNKS)),
             pltpu.SemaphoreType.DMA((CHUNKS,)),
             pltpu.SemaphoreType.DMA((1,)),
+            pltpu.SemaphoreType.DMA((6,)),
         ],
         compiler_params=pltpu.CompilerParams(
             collective_id=0, has_side_effects=True, vmem_limit_bytes=52 * 1024 * 1024
         ),
-    )(turned, filter_taps, keep, *(jnp.asarray(table) for table in dft_tables(channels)))
+    )(turned, *tables)
 
 
 def body(n_freq, voltages, filter_taps, station_flags):
@@ -484,7 +506,7 @@
     totals = correlate(n_freq, voltages.transpose(1, 0, 2), filter_taps, keep)
     counts = jnp.dot(own_flags, signal_flags.T, precision=lax.Precision.HIGHEST)
     denominator = AVG * jnp.maximum(counts, 1.0)
-    return totals / denominator[None]
+    return totals.astype(jnp.float32) / denominator[None]
 
 
 def solution(mesh):

time: 169 us -> 166 us (0.982)
  no operation moved by 1% of the time
where the time goes in v3:
time: 166 us
  Pallas kernels  149 us (90%)
  local copies, waits for them, and re-layouts  8.86 us (5%)
  other arithmetic  7.54 us (5%)
    pallas_call x1, Pallas kernels, correlate(): pl.pallas_call(functools.partial(correlate_kernel, n), out_shape=jax.Shap...  149 us
    unnamed x11, local copies, waits for them, and re-layouts  8.52 us
    div x1, other arithmetic, body(): return totals.astype(jnp.float32) / denominator[None]  6.82 us

profile of v3, /device:TPU:0, one launch (start us, length us, event | category | flops | bytes accessed | tf_op | source)
XLA Modules:
  0.0 165.6 jit_solution(3187938106780091270)
XLA Ops:
  0.0 0.7 convert_element_type.15
  0.7 0.1 copy.9
  0.8 0.1 broadcast_in_dim.4
  0.9 0.4 fusion
  1.4 0.1 convert_element_type.18.refs_1_
  1.5 4.2 %copy.11 = bf16[128,2,4096]{2,0,1:T(8,128)(2,1)} copy(bf16[128,2,4096]{2,1,0:T(2,128)(2,1)} %param.7) | data formatting | bytes 4194304 | tf_op args[0]
  5.7 0.0 copy-start
  5.7 0.9 copy-done
  6.7 0.0 copy-start.1
  6.7 0.9 copy-done.1
  7.6 0.0 copy-start.2
  7.6 0.9 copy-done.2
  8.6 0.0 copy-start.3
  8.6 0.7 copy-done.3
  9.3 0.0 copy-start.4
  9.3 0.7 copy-done.4
  10.0 148.8 %shard_map.73 = bf16[32,128,512]{2,1,0:T(8,128)(2,1)} custom-call(bf16[2,128,4096]{2,1,0:T(8,128)(2,1)} %bitcast.5, f32[16,4096]{1,0:T(8,128)S(1)} %copy-done, bf16[16,256]{1,0:T(8,128)(2,1)S(1)} %convert_element_type.18.refs_1_, f32[16,256]{1,0:T(8,128)S(1)} %copy-done.4, f32[16,256]{1,0:T(8,128)S(1)} %copy-done.3, bf16[256,512]{1,0:T(8,128)(2,1)S(1)} %copy-done.2, ...), custom_call_target="tpu_custom_call" | custom-call | tf_op jit(solution)/shard_map/pallas_call | solution.py:464
  158.8 6.8 %convert_divide_fusion = f32[32,128,512]{2,1,0:T(8,128)} fusion(bf16[32,128,512]{2,1,0:T(8,128)(2,1)} %shard_map.73, f32[128,512]{1,0:T(8,128)S(1)} %fusion), kind=kLoop, calls=%fused_computation | loop fusion | flops 4194304 | bytes 12845056 | tf_op jit(solution)/shard_map/div | solution.py:509
  (2 shorter events, 0.0 us)
Async XLA Ops:
  5.7 0.9 copy-start
  6.7 0.9 copy-start.1
  7.6 0.9 copy-start.2
  8.6 0.7 copy-start.3
  9.3 0.7 copy-start.4
